TPU v7x, 128 devices: a whole 4x4x4 slice. The times are simulated.
128 devices in a mesh: wide: 16 (over z, x), narrow: 8 (over y, core).
Axes of the slice: x: 4, y: 4, z: 4, core: 2. Of those that a mesh axis runs over, the one named last changes fastest.
Arguments:
- start_block: float32 [64, 6, 256, 512], P('narrow', None, 'wide'), may hold values from -6 to 6
- center_block: float32 [6, 6, 256, 512], P(None, None, 'wide'), may hold values from -0.1 to 13, as said below
- forward_blocks: float32 [4, 6, 6, 256, 512], P(None, None, None, 'wide'), may hold values from -0.1 to 0.1
- filter_cut: float32 [1], replicated, may hold values from 6 to 8
- filter_top: float32 [1], replicated, may hold values from 19 to 22
Outputs:
- basis: float32 [64, 6, 256, 512], P('narrow', None, 'wide')
- projected: float32 [64, 64], replicated
Inputs may be any that keep to these rules, and one draw needn't show every extreme that they name: center_block[i, j] equals center_block[j, i] at every node; its diagonal entries lie in 6.5 to 13 and its other entries in -0.1 to 0.1.
All inputs are finite; a program needn't handle non-finite values.
Results may differ from a plain program's by a relative error of at most 0.0003.
Values sent between devices are 32-bit elements; how exact they have to be, the bound alone decides.
A program may use at most 128 MiB of HBM per device.

v0:
```python
import jax
import jax.numpy as jnp
from jax import lax
from jax.experimental import pallas as pl
from jax.experimental.pallas import tpu as pltpu
from jax.sharding import PartitionSpec as P

MESH = pl.DeviceIdType.MESH
HIGHEST = lax.Precision.HIGHEST
F32 = jnp.float32
BF16 = jnp.bfloat16
OFFSETS = ((0, 1), (1, -1), (1, 0), (1, 1))
NW, NN = 16, 8
ML, J, Q = 8, 6, 4
MB = 4
NB = ML // MB
PB = MB * J
PL = ML * J
VR_ = 32
FR_ = 24
VSZ = PL * Q * VR_
UNKNOWNS = 786432.0
SHIFTED = ((0, 1), (1, -1), (3, 1))


def lanes(rows=8):
    return lax.broadcasted_iota(jnp.int32, (rows, 128), 1)


def from_left(tiles):
    rolled = [pltpu.roll(t, 1, 1) for t in tiles]
    mask = lanes(tiles[0].shape[0]) == 0
    return [jnp.where(mask, rolled[(q - 1) % Q], rolled[q]) for q in range(Q)]


def from_right(tiles):
    rolled = [pltpu.roll(t, 127, 1) for t in tiles]
    mask = lanes(tiles[0].shape[0]) == 127
    return [jnp.where(mask, rolled[(q + 1) % Q], rolled[q]) for q in range(Q)]


def groups(count):
    return [(at, min(8, count - at)) for at in range(0, count, 8)]


def kernel(x, cen, fwd, cut, top, out, proj,
           vc, vl, vr, cv, fv, sh, cs, ch, hs, hr, eps, epr, mc, ml, mr, k5, wm, s, rb,
           a0, a1, ps, a2, pt, a3,
           ldsem, hss, hrs, css, crs, mss, mrs, ess, ers, a1s, a1r, a2s, a2r, a3s, a3r, bss, brs, locs):
    w, n = lax.axis_index("wide"), lax.axis_index("narrow")
    qme, gme = n // 2, n % 2

    vc6 = vc.reshape(2, ML, J, Q, VR_, 128)
    vc4 = vc.reshape(2 * PL, Q, VR_, 128)
    cv5 = cv.reshape(J, J, Q, 16, 128)
    fv6 = fv.reshape(4, J, J, Q, FR_, 128)
    mc4 = mc.reshape(NN, PL, 16, 128)
    rb5 = rb.reshape(NN, ML, J, 8, 128)

    xl, cl, fl = [], [], []
    for q in range(Q):
        col = pl.ds(128 * q, 128)
        xl.append(pltpu.make_async_copy(x.at[:, :, :, col], vc6.at[0, :, :, q, pl.ds(8, 16)], ldsem.at[q]))
        cl.append(pltpu.make_async_copy(cen.at[:, :, :, col], cv5.at[:, :, q], ldsem.at[4 + q]))
        fl.append(pltpu.make_async_copy(fwd.at[:, :, :, :, col], fv6.at[:, :, :, q, pl.ds(8, 16)], ldsem.at[8 + q]))
    for c in xl + fl + cl:
        c.start()

    barrier = pltpu.get_barrier_semaphore()
    for d in range(1, NN):
        pl.semaphore_signal(barrier, inc=1, device_id=(w, (n + d) % NN), device_id_type=MESH)
    for d in range(1, NW):
        pl.semaphore_signal(barrier, inc=1, device_id=((w + d) % NW, n), device_id_type=MESH)

    zero = jnp.zeros((8, 128), F32)

    def clear(p, _):
        for at in (8, 16):
            vc[pl.ds(pl.multiple_of(VSZ + p * VR_, 8) + at, 8), :] = zero
        return 0

    lax.fori_loop(0, PL * Q, clear, 0)

    @pl.when(w == 0)
    def _():
        for lv in range(3):
            for b in range(NB):
                hr[lv, b, 0] = jnp.zeros((Q * PB, 128), F32)
        ch[...] = jnp.zeros_like(ch)

    @pl.when(w == NW - 1)
    def _():
        for lv in range(4):
            for b in range(NB):
                hr[lv, b, 1] = jnp.zeros((Q * PB, 128), F32)

    up_dev, down_dev = (lax.rem(w + NW - 1, NW), n), (lax.rem(w + 1, NW), n)

    def halo(lv, b, side):
        return pltpu.make_async_remote_copy(
            src_ref=hs.at[lv, b, side], dst_ref=hr.at[lv, b, side], send_sem=hss.at[lv, b, side],
            recv_sem=hrs.at[lv, b, side], device_id=down_dev if side == 0 else up_dev, device_id_type=MESH)

    def extract(lv, b, buf, both):
        base = buf * VSZ + b * (PB * Q * VR_)
        for q in range(Q):
            for at, cnt in groups(PB):
                off = base + (at * Q + q) * VR_
                if both:
                    hs[lv, b, 0, pl.ds(q * PB + at, cnt), :] = vc[pl.ds(off + 23, cnt, stride=Q * VR_), :]
                hs[lv, b, 1, pl.ds(q * PB + at, cnt), :] = vc[pl.ds(off + 8, cnt, stride=Q * VR_), :]

    def send_halo(lv, b):
        @pl.when(w < NW - 1)
        def _():
            halo(lv, b, 0).start()

        @pl.when(w > 0)
        def _():
            halo(lv, b, 1).start()

    def shift_own(b, buf):
        def body(p, _):
            src = pl.multiple_of(buf * VSZ + (b * PB + p) * (Q * VR_), 8)
            dst = pl.multiple_of((b * PB + p) * (Q * VR_), 8)
            for g in range(2):
                tiles = [vc[pl.ds(src + q * VR_ + 8 + 8 * g, 8), :] for q in range(Q)]
                for q, t in enumerate(from_left(tiles)):
                    vl[pl.ds(dst + q * VR_ + 8 + 8 * g, 8), :] = t
                for q, t in enumerate(from_right(tiles)):
                    vr[pl.ds(dst + q * VR_ + 8 + 8 * g, 8), :] = t
            return 0

        lax.fori_loop(0, PB, body, 0)

    def unpack_halo(lv, b, buf):
        for side, row in ((0, 7), (1, 24)):
            for at, cnt in groups(PB):
                tiles = [hr[lv, b, side, pl.ds(q * PB + at, cnt), :] for q in range(Q)]
                base = (b * PB + at) * (Q * VR_)
                for ref, off, vals in ((vc, buf * VSZ, tiles), (vl, 0, from_left(tiles)), (vr, 0, from_right(tiles))):
                    for q in range(Q):
                        ref[pl.ds(off + base + q * VR_ + row, cnt, stride=Q * VR_), :] = vals[q]

    for c in xl:
        c.wait()
    for b in range(NB):
        extract(0, b, 0, True)
    pl.semaphore_wait(barrier, NN + NW - 2)
    for b in range(NB):
        send_halo(0, b)

    for c in fl:
        c.wait()
    for q in range(Q):
        for f in range(1, 4):
            for at, cnt in groups(36):
                cs[q, pl.ds((f - 1) * 36 + at, cnt), :] = fv[pl.ds(((f * 36 + at) * Q + q) * FR_ + 23, cnt, stride=Q * FR_), :]
    coef_halo = pltpu.make_async_remote_copy(
        src_ref=cs, dst_ref=ch, send_sem=css, recv_sem=crs, device_id=down_dev, device_id_type=MESH)

    @pl.when(w < NW - 1)
    def _():
        coef_halo.start()

    for b in range(NB):
        shift_own(b, 0)
    for at3, (f, step) in enumerate(SHIFTED):
        def body(p, _, at3=at3, f=f, step=step):
            src = pl.multiple_of((f * 36 + p) * (Q * FR_), 8)
            dst = pl.multiple_of((at3 * 36 + p) * (Q * FR_), 8)
            for g in range(2):
                tiles = [fv[pl.ds(src + q * FR_ + 8 + 8 * g, 8), :] for q in range(Q)]
                moved = from_left(tiles) if step == 1 else from_right(tiles)
                for q in range(Q):
                    sh[pl.ds(dst + q * FR_ + 8 + 8 * g, 8), :] = moved[q]
            return 0

        lax.fori_loop(0, 36, body, 0)

    @pl.when(w > 0)
    def _():
        coef_halo.wait_recv()

    for at, cnt in groups(36):
        for f, ref, slot, move in ((1, sh, 1, from_right), (2, fv, 2, None), (3, sh, 2, from_left)):
            tiles = [ch[q, pl.ds((f - 1) * 36 + at, cnt), :] for q in range(Q)]
            tiles = tiles if move is None else move(tiles)
            for q in range(Q):
                ref[pl.ds(((slot * 36 + at) * Q + q) * FR_ + 7, cnt, stride=Q * FR_), :] = tiles[q]
    for c in cl:
        c.wait()

    middle = 0.5 * (cut[0] + top[0])
    half_width = 0.5 * (top[0] - cut[0])

    stencil = [(cv, 16, 0, 0, False, 0, 0)]
    for f, (dr, dc) in enumerate(OFFSETS):
        stencil.append((fv, FR_, f * 36, 8, False, dc, dr))
    for ref, slot, (dr, dc) in ((sh, 0, (0, 1)), (sh, 1, (1, -1)), (fv, 2, (1, 0)), (sh, 2, (1, 1))):
        stencil.append((ref, FR_, slot * 36, 8 - dr, True, -dc, -dr))

    def apply(lv, b):
        cur = lax.rem(lv, 2) * VSZ
        nxt = VSZ - cur
        scale = jnp.where(lv == 0, 1.0, 2.0) / half_width
        vb = b * (PB * Q * VR_)

        def body(q, _):
            vq = q * VR_
            for g in range(2):
                acc = [[None] * J for _ in range(MB)]
                for ref, slot_rows, plane0, row0, transposed, dc, dr in stencil:
                    for j in range(J):
                        src = {0: vc, 1: vr, -1: vl}[dc]
                        base = pl.multiple_of(vb + vq + (cur if dc == 0 else 0), 8)
                        vs = [src[pl.ds(base + (m * J + j) * (Q * VR_) + 8 + 8 * g + dr, 8), :] for m in range(MB)]
                        for i in range(J):
                            plane = plane0 + (j * J + i if transposed else i * J + j)
                            cbase = pl.multiple_of(q * slot_rows, 8)
                            cf = ref[pl.ds(cbase + plane * (Q * slot_rows) + row0 + 8 * g, 8), :]
                            for m in range(MB):
                                term = cf * vs[m]
                                acc[m][i] = term if acc[m][i] is None else acc[m][i] + term
                for m in range(MB):
                    for i in range(J):
                        off = vb + vq
                        at = (m * J + i) * (Q * VR_) + 8 + 8 * g
                        here = vc[pl.ds(pl.multiple_of(off + cur, 8) + at, 8), :]
                        there = pl.ds(pl.multiple_of(off + nxt, 8) + at, 8)
                        vc[there, :] = (acc[m][i] - middle * here) * scale - vc[there, :]
            return 0

        lax.fori_loop(0, Q, body, 0)

    def main_copy(b, dst, sender):
        return pltpu.make_async_remote_copy(
            src_ref=vc4.at[pl.ds(PL + b * PB, PB), dst // 2, pl.ds(pl.multiple_of(8 + 8 * lax.rem(dst, 2), 8), 8)],
            dst_ref=mc4.at[sender, pl.ds(b * PB, PB), pl.ds(0, 8)],
            send_sem=mss.at[b, dst], recv_sem=mrs.at[b, sender], device_id=(w, dst), device_id_type=MESH)

    def own_main(b):
        return pltpu.make_async_copy(
            vc4.at[pl.ds(PL + b * PB, PB), qme, pl.ds(pl.multiple_of(8 + 8 * gme, 8), 8)],
            mc4.at[n, pl.ds(b * PB, PB), pl.ds(0, 8)], locs.at[b])

    def edge_copy(b, dst, sender):
        return pltpu.make_async_remote_copy(
            src_ref=eps.at[b, dst], dst_ref=epr.at[b, sender], send_sem=ess.at[b, dst], recv_sem=ers.at[b, sender],
            device_id=(w, dst), device_id_type=MESH)

    def own_edge(b):
        return pltpu.make_async_copy(eps.at[b, n], epr.at[b, n], locs.at[NB + b])

    def step(t, _):
        lv, b = t // NB, lax.rem(t, NB)
        buf = lax.rem(lv, 2)

        @pl.when(w > 0)
        def _():
            halo(lv, b, 0).wait_recv()

        @pl.when(w < NW - 1)
        def _():
            halo(lv, b, 1).wait_recv()

        unpack_halo(lv, b, buf)
        apply(lv, b)
        extract(lv + 1, b, 1 - buf, True)

        @pl.when(lv < 2)
        def _():
            send_halo(lv + 1, b)
            shift_own(b, 1 - buf)

        @pl.when(lv == 2)
        def _():
            @pl.when(w > 0)
            def _():
                halo(3, b, 1).start()

            for d in (4, 3, 5, 2, 6, 7, 1):
                dst = lax.rem(n + d, NN)
                main_copy(b, dst, n).start()
            own_main(b).start()

        return 0

    lax.fori_loop(0, 3 * NB, step, 0)

    lane = lanes()

    def edges(b, _):
        @pl.when(w < NW - 1)
        def _():
            halo(3, b, 1).wait_recv()

        def body(q, _):
            right, left = lax.rem(q + 1, Q), lax.rem(q + 3, Q)
            base = VSZ + b * (PB * Q * VR_)
            for g in range(2):
                dst = q * 2 + g
                pack = zero
                for p in range(PB):
                    at = p * (Q * VR_) + 8 + 8 * g
                    vright = vc[pl.ds(pl.multiple_of(base + right * VR_, 8) + at, 8), :]
                    vleft = vc[pl.ds(pl.multiple_of(base + left * VR_, 8) + at, 8), :]
                    pack = jnp.where(lane == p, vright if p == 0 else pltpu.roll(vright, p, 1), pack)
                    pack = jnp.where(lane == 32 + p, pltpu.roll(vleft, 33 + p, 1), pack)
                for k in range(PB // 8):
                    def row(at_q):
                        if g == 0:
                            off = pl.multiple_of(base + at_q * VR_, 8) + 8 * k * (Q * VR_) + 16
                            return vc[pl.ds(off, 8, stride=Q * VR_), :]
                        return hr[3, b, 1, pl.ds(pl.multiple_of(at_q * PB, 8) + 8 * k, 8), :]

                    eps[b, dst, pl.ds(8 * k, 8), :] = row(q)
                    pack = jnp.where(lane == 64 + k, pltpu.roll(row(right), 64 + k, 1), pack)
                    pack = jnp.where(lane == 72 + k, pltpu.roll(row(left), 73 + k, 1), pack)
                eps[b, dst, pl.ds(PB, 8), :] = pack
            return 0

        lax.fori_loop(0, Q, body, 0)
        for d in (4, 3, 5, 2, 6, 7, 1):
            edge_copy(b, lax.rem(n + d, NN), n).start()
        own_edge(b).start()
        return 0

    lax.fori_loop(0, NB, edges, 0)

    def own_coef(p, _):
        src = pl.multiple_of(p * (Q * 16) + qme * 16 + 8 * gme, 8)
        k5[pl.ds(pl.multiple_of(p * 8, 8), 8), :] = 0.5 * cv[pl.ds(src, 8), :]
        return 0

    def own_forward(p, _):
        src = pl.multiple_of(p * (Q * FR_) + qme * FR_ + 8 + 8 * gme, 8)
        k5[pl.ds(pl.multiple_of(288 + p * 8, 8), 8), :] = fv[pl.ds(src, 8), :]
        return 0

    lax.fori_loop(0, 36, own_coef, 0)
    lax.fori_loop(0, 144, own_forward, 0)

    def unpack(b, src):
        base = pl.multiple_of((src * PL + b * PB) * 16, 8)
        pack = epr[b, src, pl.ds(PB, 8), :]
        for p in range(PB):
            v = mc[pl.ds(base + p * 16, 8), :]
            mr[pl.ds(base + p * 16, 8), :] = jnp.where(lane == 127, pltpu.roll(pack, 127 - p, 1), pltpu.roll(v, 127, 1))
            ml[pl.ds(base + p * 16, 8), :] = jnp.where(lane == 0, pltpu.roll(pack, 96 - p, 1), pltpu.roll(v, 1, 1))
        for k in range(PB // 8):
            h = epr[b, src, pl.ds(8 * k, 8), :]
            there = pl.ds(base + 128 * k + 8, 8, stride=16)
            mc[there, :] = h
            mr[there, :] = jnp.where(lane == 127, pltpu.roll(pack, 63 - k, 1), pltpu.roll(h, 127, 1))
            ml[there, :] = jnp.where(lane == 0, pltpu.roll(pack, 56 - k, 1), pltpu.roll(h, 1, 1))

    half_stencil = ((mc, 0), (mr, 0), (ml, 1), (mc, 1), (mr, 1))

    def half_apply(b, src):
        base = pl.multiple_of((src * PL + b * PB) * 16, 8)
        wbase = pl.multiple_of((src * PL + b * PB) * 8, 8)
        acc = [[None] * J for _ in range(MB)]
        for f, (ref, dr) in enumerate(half_stencil):
            for j in range(J):
                vs = [ref[pl.ds(base + (m * J + j) * 16 + dr, 8), :] for m in range(MB)]
                for i in range(J):
                    cf = k5[pl.ds((f * 36 + i * J + j) * 8, 8), :]
                    for m in range(MB):
                        term = cf * vs[m]
                        acc[m][i] = term if acc[m][i] is None else acc[m][i] + term
        for m in range(MB):
            for i in range(J):
                wm[pl.ds(wbase + (m * J + i) * 8, 8), :] = acc[m][i]

    def meet(t, _):
        b, d = t // NN, lax.rem(t, NN)
        src = lax.rem(n + d, NN)

        @pl.when(d == 0)
        def _():
            own_main(b).wait()
            own_edge(b).wait()

        @pl.when(d > 0)
        def _():
            main_copy(b, n, src).wait_recv()
            edge_copy(b, n, src).wait_recv()

        unpack(b, src)
        half_apply(b, src)
        return 0

    lax.fori_loop(0, NB * NN, meet, 0)

    def split(v):
        hi = v.astype(BF16)
        return hi, (v - hi.astype(F32)).astype(BF16)

    for j in range(J):
        for r in range(8):
            col = pl.ds((j * 8 + r) * 128, 128)
            y = jnp.concatenate([mc[pl.ds((k * PL + j) * 16 + r, 8, stride=J * 16), :] for k in range(NN)], axis=0)
            z = jnp.concatenate([wm[pl.ds((k * PL + j) * 8 + r, 8, stride=J * 8), :] for k in range(NN)], axis=0)
            yhi, ylo = split(y)
            zhi, zlo = split(z)
            s[pl.ds(0, 64), col] = yhi
            s[pl.ds(64, 64), col] = zhi
            s[pl.ds(128, 64), col] = ylo
            s[pl.ds(192, 64), col] = zlo
    total = jnp.zeros((128, 256), F32)
    for k in range(12):
        col = pl.ds(k * 512, 512)
        left = jnp.concatenate([s[pl.ds(0, 64), col], s[pl.ds(128, 64), col]], axis=0)
        total = total + lax.dot_general(left, s[:, col], (((1,), (1,)), ((), ())), preferred_element_type=F32)
    a0[...] = ((total[0:64, 0:128] + (total[64:128, 0:128] + total[0:64, 128:256])) + total[64:128, 128:256]) / UNKNOWNS

    def piece1(dst, sender):
        return pltpu.make_async_remote_copy(
            src_ref=a0.at[pl.ds(pl.multiple_of(dst * 8, 8), 8)], dst_ref=a1.at[sender], send_sem=a1s.at[dst],
            recv_sem=a1r.at[sender], device_id=(w, dst), device_id_type=MESH)

    def piece2(dst, sender):
        return pltpu.make_async_remote_copy(
            src_ref=ps, dst_ref=a2.at[sender], send_sem=a2s.at[dst], recv_sem=a2r.at[sender],
            device_id=(dst, n), device_id_type=MESH)

    def piece3(dst, sender):
        return pltpu.make_async_remote_copy(
            src_ref=pt, dst_ref=a3.at[sender], send_sem=a3s.at[dst], recv_sem=a3r.at[sender],
            device_id=(w, dst), device_id_type=MESH)

    def exchange(piece, count, me):
        for d in range(1, count):
            piece(lax.rem(me + d, count), me).start()

    def collect(piece, count, me):
        for d in range(1, count):
            piece(me, lax.rem(me + d, count)).wait_recv()

    exchange(piece1, NN, n)
    a1[n] = a0[pl.ds(pl.multiple_of(n * 8, 8), 8), :]
    collect(piece1, NN, n)
    ps[...] = sum(a1[k] for k in range(1, NN)) + a1[0]
    exchange(piece2, NW, w)
    a2[w] = ps[...]
    collect(piece2, NW, w)
    pt[...] = sum(a2[k] for k in range(1, NW)) + a2[0]
    exchange(piece3, NN, n)
    a3[n] = pt[...]
    collect(piece3, NN, n)
    gz = jnp.concatenate([a3[k] for k in range(NN)], axis=0)

    lane64 = lanes(64)
    row64 = lax.broadcasted_iota(jnp.int32, (64, 128), 0)
    work = jnp.where(lane64 < 64, gz, (lane64 - 64 == row64).astype(F32))
    for k in range(64):
        pivot = work[k:k + 1, k:k + 1]
        factor = jnp.where(row64 > k, work[:, k:k + 1] / pivot, 0.0)
        work = work - factor * work[k:k + 1, :]
    diag = jnp.sum(jnp.where(lane64 == row64, work, 0.0), axis=1, keepdims=True)
    work = work * lax.rsqrt(diag)
    turned = pltpu.roll(work, 64, 1)
    twice = jnp.where(lane64 < 64, turned, work)
    mhi, mlo = split(twice)
    mix = jnp.concatenate([mhi, mlo], axis=0)

    def back(dst):
        return pltpu.make_async_remote_copy(
            src_ref=rb5.at[dst],
            dst_ref=out.at[:, :, pl.ds(pl.multiple_of(8 * gme, 8), 8), pl.ds(pl.multiple_of(128 * qme, 128), 128)],
            send_sem=bss.at[dst], recv_sem=brs.at[n], device_id=(w, dst), device_id_type=MESH)

    def back_arrival(sender):
        return pltpu.make_async_remote_copy(
            src_ref=rb5.at[sender],
            dst_ref=out.at[:, :, pl.ds(pl.multiple_of(8 * lax.rem(sender, 2), 8), 8),
                           pl.ds(pl.multiple_of(128 * (sender // 2), 128), 128)],
            send_sem=bss.at[sender], recv_sem=brs.at[sender], device_id=(w, sender), device_id_type=MESH)

    for tile in range(24):
        col = pl.ds(tile * 256, 256)
        right = jnp.concatenate([s[pl.ds(0, 64), col], s[pl.ds(128, 64), col]], axis=0)
        both = jnp.dot(mix, right, preferred_element_type=F32)
        basis = both[0:64] + both[64:128]
        for half in range(2):
            j, r = divmod(tile * 2 + half, 8)
            for k in range(NN):
                rb[pl.ds((k * PL + j) * 8 + r, 8, stride=J * 8), :] = basis[8 * k:8 * k + 8, 128 * half:128 * half + 128]
    for d in (4, 3, 5, 2, 6, 7, 1):
        back(lax.rem(n + d, NN)).start()
    own_back = pltpu.make_async_copy(
        rb5.at[n],
        out.at[:, :, pl.ds(pl.multiple_of(8 * gme, 8), 8), pl.ds(pl.multiple_of(128 * qme, 128), 128)],
        locs.at[2 * NB])
    own_back.start()

    minv = jnp.where(lane64 < 64, turned, 0.0)[:, 0:64]
    zmat = pltpu.roll(gz, 64, 1)[:, 0:64]
    half = jnp.dot(minv, zmat, precision=HIGHEST, preferred_element_type=F32) + lax.dot_general(
        minv, zmat, (((1,), (1,)), ((), ())), precision=HIGHEST, preferred_element_type=F32)
    proj[...] = lax.dot_general(half, minv, (((1,), (1,)), ((), ())), precision=HIGHEST, preferred_element_type=F32)

    for lv in range(3):
        for b in range(NB):
            @pl.when(w < NW - 1)
            def _():
                halo(lv, b, 0).wait_send()
    for lv in range(4):
        for b in range(NB):
            @pl.when(w > 0)
            def _():
                halo(lv, b, 1).wait_send()

    @pl.when(w < NW - 1)
    def _():
        coef_halo.wait_send()

    for d in range(1, NN):
        dst = lax.rem(n + d, NN)
        for b in range(NB):
            main_copy(b, dst, n).wait_send()
            edge_copy(b, dst, n).wait_send()
        piece1(dst, n).wait_send()
        piece3(dst, n).wait_send()
    for d in range(1, NW):
        piece2(lax.rem(w + d, NW), w).wait_send()
    own_back.wait()
    for d in range(1, NN):
        other = lax.rem(n + d, NN)
        back(other).wait_send()
        back_arrival(other).wait_recv()


def local(start_block, center_block, forward_blocks, filter_cut, filter_top):
    dma = pltpu.SemaphoreType.DMA
    vm = lambda *shape: pltpu.VMEM(shape, F32)
    anyspace = pl.BlockSpec(memory_space=pl.ANY)
    smem = pl.BlockSpec(memory_space=pltpu.SMEM)
    return pl.pallas_call(
        kernel,
        out_shape=(jax.ShapeDtypeStruct((ML, J, 16, 512), F32), jax.ShapeDtypeStruct((64, 64), F32)),
        in_specs=[anyspace, anyspace, anyspace, smem, smem],
        out_specs=(anyspace, pl.BlockSpec(memory_space=pltpu.VMEM)),
        scratch_shapes=[
            vm(2 * VSZ, 128), vm(VSZ, 128), vm(VSZ, 128),
            vm(36 * Q * 16, 128), vm(144 * Q * FR_, 128), vm(108 * Q * FR_, 128),
            vm(Q, 112, 128), vm(Q, 112, 128),
            vm(4, NB, 2, Q * PB, 128), vm(4, NB, 2, Q * PB, 128),
            vm(NB, NN, PB + 8, 128), vm(NB, NN, PB + 8, 128),
            vm(NN * PL * 16, 128), vm(NN * PL * 16, 128), vm(NN * PL * 16, 128),
            vm(180 * 8, 128), vm(NN * PL * 8, 128), pltpu.VMEM((256, 6144), BF16), vm(NN * PL * 8, 128),
            vm(64, 128), vm(NN, 8, 128), vm(8, 128), vm(NW, 8, 128), vm(8, 128), vm(NN, 8, 128),
            dma((12,)), dma((4, NB, 2)), dma((4, NB, 2)), dma(()), dma(()),
            dma((NB, NN)), dma((NB, NN)), dma((NB, NN)), dma((NB, NN)),
            dma((NN,)), dma((NN,)), dma((NW,)), dma((NW,)), dma((NN,)), dma((NN,)), dma((NN,)), dma((NN,)),
            dma((2 * NB + 1,)),
        ],
        compiler_params=pltpu.CompilerParams(
            collective_id=0, has_side_effects=True, vmem_limit_bytes=60 * 1024 * 1024),
    )(start_block, center_block, forward_blocks, filter_cut, filter_top)


def solution(mesh):
    in_specs = (
        P("narrow", None, "wide", None),
        P(None, None, "wide", None),
        P(None, None, None, "wide", None),
        P(),
        P(),
    )
    out_specs = (P("narrow", None, "wide", None), P())
    return jax.shard_map(local, mesh=mesh, in_specs=in_specs, out_specs=out_specs, check_vma=False)
```

profile of v0, /device:TPU:0, one launch (start us, length us, event | category | flops | bytes accessed | tf_op | source)
XLA Modules:
  0.0 121.9 jit_solution(16612311326944407424)
XLA Ops:
  1.9 116.5 %shard_map.68 = (f32[8,6,16,512]{3,2,1,0:T(8,128)}, f32[64,64]{1,0:T(8,128)}) custom-call(f32[8,6,16,512]{3,2,1,0:T(8,128)} %x.1, f32[6,6,16,512]{3,2,1,0:T(8,128)} %cen.1, f32[4,6,6,16,512]{4,3,2,1,0:T(8,128)} %fwd.1, f32[1]{0:T(128)S(6)} %copy.9.cut, f32[1]{0:T(128)S(6)} %copy.10.top), custom_call_target="tpu_custom_call" | custom-call | tf_op jit(solution)/shard_map/pallas_call | solution.py:540
  118.5 0.0 copy-start
  118.5 2.8 %copy.11 = f32[8,6,16,512]{3,2,1,0:T(8,128)} copy(f32[8,6,16,512]{3,2,1,0:T(8,128)} %get-tuple-element.4) | data formatting | bytes 3145728
  121.2 0.0 copy-done
  121.3 0.6 copy.12
Async XLA Ops:
  118.5 2.8 %copy-start = (f32[64,64]{1,0:T(8,128)S(1)}, f32[64,64]{1,0:T(8,128)}, u32[]{:S(2)}) copy-start(f32[64,64]{1,0:T(8,128)} %get-tuple-element.5) | copy-start | bytes 49156
where the time goes:
time: 122 us
  Pallas kernels  117 us (96%)
  local copies, waits for them, and re-layouts  3.39 us (3%)
  between operations  1.94 us (2%)
    pallas_call x1, Pallas kernels, local(): pl.pallas_call(kernel, out_shape=(jax.ShapeDtypeStruct((ML, J, 16, 512),...  117 us
    unnamed x4, local copies, waits for them, and re-layouts  3.39 us

commit v1 on v0

v1 whole, which is shorter than its diff:
```python
import jax
import jax.numpy as jnp
from jax import lax
from jax.experimental import pallas as pl
from jax.experimental.pallas import tpu as pltpu
from jax.sharding import PartitionSpec as P

MESH = pl.DeviceIdType.MESH
HIGHEST = lax.Precision.HIGHEST
F32 = jnp.float32
BF16 = jnp.bfloat16
OFFSETS = ((0, 1), (1, -1), (1, 0), (1, 1))
NW, NN = 16, 8
ML, J, Q = 8, 6, 4
MB = 4
NB = ML // MB
PB = MB * J
PL = ML * J
ER = (PB + 7) // 8 * 8
VR_ = 32
FR_ = 24
VSZ = PL * Q * VR_
UNKNOWNS = 786432.0
SHIFTED = ((0, 1), (1, -1), (3, 1))


def lanes(rows=8):
    return lax.broadcasted_iota(jnp.int32, (rows, 128), 1)


def from_left(tiles):
    rolled = [pltpu.roll(t, 1, 1) for t in tiles]
    mask = lanes(tiles[0].shape[0]) == 0
    return [jnp.where(mask, rolled[(q - 1) % Q], rolled[q]) for q in range(Q)]


def from_right(tiles):
    rolled = [pltpu.roll(t, 127, 1) for t in tiles]
    mask = lanes(tiles[0].shape[0]) == 127
    return [jnp.where(mask, rolled[(q + 1) % Q], rolled[q]) for q in range(Q)]


def groups(count):
    return [(at, min(8, count - at)) for at in range(0, count, 8)]


def kernel(x, cen, fwd, cut_hbm, top_hbm, out, proj,
           cut, top, vc, vl, vr, cv, fv, sh, cs, ch, hs, hr, eps, epr, mc, ml, mr, k5, wm, s, rb,
           a0, a1, ps, a2, pt, a3, pv, z0, z1, zp, z2,
           ldsem, hss, hrs, css, crs, mss, mrs, ess, ers, a1s, a1r, a2s, a2r, a3s, a3r, z1s, z1r, z2s, z2r, bss, brs, locs):
    w, n = lax.axis_index("wide"), lax.axis_index("narrow")
    qme, gme = n // 2, n % 2

    vc6 = vc.reshape(2, ML, J, Q, VR_, 128)
    vc4 = vc.reshape(2 * PL, Q, VR_, 128)
    cv5 = cv.reshape(J, J, Q, 16, 128)
    fv6 = fv.reshape(4, J, J, Q, FR_, 128)
    mc4 = mc.reshape(NN, PL, 16, 128)
    rb5 = rb.reshape(NN, ML, J, 8, 128)

    barrier = pltpu.get_barrier_semaphore()
    for d in range(1, NN):
        pl.semaphore_signal(barrier, inc=1, device_id=(w, (n + d) % NN), device_id_type=MESH)
    for d in range(1, NW):
        pl.semaphore_signal(barrier, inc=1, device_id=((w + d) % NW, n), device_id_type=MESH)

    xl, cl, fl = [], [], []
    for q in range(Q):
        col = pl.ds(128 * q, 128)
        xl.append(pltpu.make_async_copy(x.at[:, :, :, col], vc6.at[0, :, :, q, pl.ds(8, 16)], ldsem.at[q]))
        cl.append(pltpu.make_async_copy(cen.at[:, :, :, col], cv5.at[:, :, q], ldsem.at[4 + q]))
        fl.append(pltpu.make_async_copy(fwd.at[:, :, :, :, col], fv6.at[:, :, :, q, pl.ds(8, 16)], ldsem.at[8 + q]))
    scalars = [pltpu.make_async_copy(cut_hbm, cut, ldsem.at[12]), pltpu.make_async_copy(top_hbm, top, ldsem.at[13])]
    for c in fl + xl + cl + scalars:
        c.start()

    zero = jnp.zeros((8, 128), F32)

    def whole(v):
        return v if v.shape[0] == 8 else jnp.concatenate([v, zero[v.shape[0]:]], axis=0)

    def clear(p, _):
        for at in (8, 16):
            vc[pl.ds(pl.multiple_of(VSZ + p * VR_, 8) + at, 8), :] = zero
        return 0

    lax.fori_loop(0, PL * Q, clear, 0, unroll=8)

    @pl.when(w == 0)
    def _():
        for lv in range(3):
            for b in range(NB):
                hr[lv, b, 0] = jnp.zeros((Q * PB, 128), F32)
        ch[...] = jnp.zeros_like(ch)

    @pl.when(w == NW - 1)
    def _():
        for lv in range(4):
            for b in range(NB):
                hr[lv, b, 1] = jnp.zeros((Q * PB, 128), F32)

    up_dev, down_dev = (lax.rem(w + NW - 1, NW), n), (lax.rem(w + 1, NW), n)

    def halo(lv, b, side):
        return pltpu.make_async_remote_copy(
            src_ref=hs.at[lv, b, side], dst_ref=hr.at[lv, b, side], send_sem=hss.at[lv, b, side],
            recv_sem=hrs.at[lv, b, side], device_id=down_dev if side == 0 else up_dev, device_id_type=MESH)

    def extract(lv, b, buf, both):
        base = buf * VSZ + b * (PB * Q * VR_)
        for q in range(Q):
            for at, cnt in groups(PB):
                off = base + (at * Q + q) * VR_
                if both:
                    hs[lv, b, 0, pl.ds(q * PB + at, cnt), :] = vc[pl.ds(off + 23, cnt, stride=Q * VR_), :]
                hs[lv, b, 1, pl.ds(q * PB + at, cnt), :] = vc[pl.ds(off + 8, cnt, stride=Q * VR_), :]

    def send_halo(lv, b):
        @pl.when(w < NW - 1)
        def _():
            halo(lv, b, 0).start()

        @pl.when(w > 0)
        def _():
            halo(lv, b, 1).start()

    def shift_own(b, buf):
        def body(p, _):
            src = pl.multiple_of(buf * VSZ + (b * PB + p) * (Q * VR_), 8)
            dst = pl.multiple_of((b * PB + p) * (Q * VR_), 8)
            for g in range(2):
                tiles = [vc[pl.ds(src + q * VR_ + 8 + 8 * g, 8), :] for q in range(Q)]
                for q, t in enumerate(from_left(tiles)):
                    vl[pl.ds(dst + q * VR_ + 8 + 8 * g, 8), :] = t
                for q, t in enumerate(from_right(tiles)):
                    vr[pl.ds(dst + q * VR_ + 8 + 8 * g, 8), :] = t
            return 0

        lax.fori_loop(0, PB, body, 0, unroll=12)

    def unpack_halo(lv, b, buf):
        for side, row in ((0, 7), (1, 24)):
            for at, cnt in groups(PB):
                tiles = [hr[lv, b, side, pl.ds(q * PB + at, cnt), :] for q in range(Q)]
                base = (b * PB + at) * (Q * VR_)
                for ref, off, vals in ((vc, buf * VSZ, tiles), (vl, 0, from_left(tiles)), (vr, 0, from_right(tiles))):
                    for q in range(Q):
                        ref[pl.ds(off + base + q * VR_ + row, cnt, stride=Q * VR_), :] = vals[q]

    for c in fl:
        c.wait()
    for q in range(Q):
        for f in range(1, 4):
            for at, cnt in groups(36):
                cs[q, pl.ds((f - 1) * 36 + at, cnt), :] = fv[pl.ds(((f * 36 + at) * Q + q) * FR_ + 23, cnt, stride=Q * FR_), :]
    for at3, (f, step) in enumerate(SHIFTED):
        def body(p, _, at3=at3, f=f, step=step):
            src = pl.multiple_of((f * 36 + p) * (Q * FR_), 8)
            dst = pl.multiple_of((at3 * 36 + p) * (Q * FR_), 8)
            for g in range(2):
                tiles = [fv[pl.ds(src + q * FR_ + 8 + 8 * g, 8), :] for q in range(Q)]
                moved = from_left(tiles) if step == 1 else from_right(tiles)
                for q in range(Q):
                    sh[pl.ds(dst + q * FR_ + 8 + 8 * g, 8), :] = moved[q]
            return 0

        lax.fori_loop(0, 36, body, 0, unroll=12)

    for c in xl:
        c.wait()
    for b in range(NB):
        extract(0, b, 0, True)
    pl.semaphore_wait(barrier, NN + NW - 2)
    for b in range(NB):
        send_halo(0, b)

    coef_halo = pltpu.make_async_remote_copy(
        src_ref=cs, dst_ref=ch, send_sem=css, recv_sem=crs, device_id=down_dev, device_id_type=MESH)

    @pl.when(w < NW - 1)
    def _():
        coef_halo.start()

    for b in range(NB):
        shift_own(b, 0)

    @pl.when(w > 0)
    def _():
        coef_halo.wait_recv()

    for at, cnt in groups(36):
        for f, ref, slot, move in ((1, sh, 1, from_right), (2, fv, 2, None), (3, sh, 2, from_left)):
            tiles = [ch[q, pl.ds((f - 1) * 36 + at, cnt), :] for q in range(Q)]
            tiles = tiles if move is None else move(tiles)
            for q in range(Q):
                ref[pl.ds(((slot * 36 + at) * Q + q) * FR_ + 7, cnt, stride=Q * FR_), :] = tiles[q]
    for c in cl + scalars:
        c.wait()

    middle = 0.5 * (cut[0] + top[0])
    half_width = 0.5 * (top[0] - cut[0])

    stencil = [(cv, 16, 0, 0, False, 0, 0)]
    for f, (dr, dc) in enumerate(OFFSETS):
        stencil.append((fv, FR_, f * 36, 8, False, dc, dr))
    for ref, slot, (dr, dc) in ((sh, 0, (0, 1)), (sh, 1, (1, -1)), (fv, 2, (1, 0)), (sh, 2, (1, 1))):
        stencil.append((ref, FR_, slot * 36, 8 - dr, True, -dc, -dr))

    def main_copy(b, dst, sender):
        return pltpu.make_async_remote_copy(
            src_ref=vc4.at[pl.ds(PL + b * PB, PB), dst // 2, pl.ds(pl.multiple_of(8 + 8 * lax.rem(dst, 2), 8), 8)],
            dst_ref=mc4.at[sender, pl.ds(b * PB, PB), pl.ds(0, 8)],
            send_sem=mss.at[b, dst], recv_sem=mrs.at[b, sender], device_id=(w, dst), device_id_type=MESH)

    def own_main(b):
        return pltpu.make_async_copy(
            vc4.at[pl.ds(PL + b * PB, PB), qme, pl.ds(pl.multiple_of(8 + 8 * gme, 8), 8)],
            mc4.at[n, pl.ds(b * PB, PB), pl.ds(0, 8)], locs.at[b])

    def apply(lv, b):
        cur = lax.rem(lv, 2) * VSZ
        nxt = VSZ - cur
        scale = jnp.where(lv == 0, 1.0, 2.0) / half_width
        vb = b * (PB * Q * VR_)

        def body(k, _):
            q = lax.rem(qme + 1 + k, Q)
            vq = q * VR_
            for g in range(2):
                acc = [[None] * J for _ in range(MB)]
                for ref, slot_rows, plane0, row0, transposed, dc, dr in stencil:
                    for j in range(J):
                        src = {0: vc, 1: vr, -1: vl}[dc]
                        base = pl.multiple_of(vb + vq + (cur if dc == 0 else 0), 8)
                        vs = [src[pl.ds(base + (m * J + j) * (Q * VR_) + 8 + 8 * g + dr, 8), :] for m in range(MB)]
                        for i in range(J):
                            plane = plane0 + (j * J + i if transposed else i * J + j)
                            cbase = pl.multiple_of(q * slot_rows, 8)
                            cf = ref[pl.ds(cbase + plane * (Q * slot_rows) + row0 + 8 * g, 8), :]
                            for m in range(MB):
                                term = cf * vs[m]
                                acc[m][i] = term if acc[m][i] is None else acc[m][i] + term
                for m in range(MB):
                    for i in range(J):
                        off = vb + vq
                        at = (m * J + i) * (Q * VR_) + 8 + 8 * g
                        here = vc[pl.ds(pl.multiple_of(off + cur, 8) + at, 8), :]
                        there = pl.ds(pl.multiple_of(off + nxt, 8) + at, 8)
                        vc[there, :] = (acc[m][i] - middle * here) * scale - vc[there, :]

            @pl.when((lv == 2) & (k < Q - 1))
            def _():
                for g in range(2):
                    main_copy(b, 2 * q + g, n).start()

            return 0

        lax.fori_loop(0, Q, body, 0)

    def edge_copy(b, dst, sender):
        return pltpu.make_async_remote_copy(
            src_ref=eps.at[b, dst], dst_ref=epr.at[b, sender], send_sem=ess.at[b, dst], recv_sem=ers.at[b, sender],
            device_id=(w, dst), device_id_type=MESH)

    def own_edge(b):
        return pltpu.make_async_copy(eps.at[b, n], epr.at[b, n], locs.at[NB + b])

    lane = lanes()

    def edges(b):
        @pl.when(w < NW - 1)
        def _():
            halo(3, b, 1).wait_recv()

        def body(q, _):
            right, left = lax.rem(q + 1, Q), lax.rem(q + 3, Q)
            base = VSZ + b * (PB * Q * VR_)
            for g in range(2):
                dst = q * 2 + g
                pack = zero
                for p in range(PB):
                    at = p * (Q * VR_) + 8 + 8 * g
                    vright = vc[pl.ds(pl.multiple_of(base + right * VR_, 8) + at, 8), :]
                    vleft = vc[pl.ds(pl.multiple_of(base + left * VR_, 8) + at, 8), :]
                    pack = jnp.where(lane == 2 * p, vright if p == 0 else pltpu.roll(vright, 2 * p, 1), pack)
                    pack = jnp.where(lane == 2 * p + 1, pltpu.roll(vleft, 2 * p + 2, 1), pack)
                for k, (first, cnt) in enumerate(groups(PB)):
                    def row(at_q):
                        if g == 0:
                            off = pl.multiple_of(base + at_q * VR_, 8) + first * (Q * VR_) + 16
                            return vc[pl.ds(off, cnt, stride=Q * VR_), :]
                        return hr[3, b, 1, pl.ds(at_q * PB + first, cnt), :]

                    eps[b, dst, pl.ds(first, cnt), :] = row(q)
                    pack = jnp.where(lane == 64 + 2 * k, pltpu.roll(whole(row(right)), 64 + 2 * k, 1), pack)
                    pack = jnp.where(lane == 65 + 2 * k, pltpu.roll(whole(row(left)), 66 + 2 * k, 1), pack)
                eps[b, dst, pl.ds(ER, 8), :] = pack
            return 0

        lax.fori_loop(0, Q, body, 0)
        for d in (4, 3, 5, 2, 6, 7, 1):
            edge_copy(b, lax.rem(n + d, NN), n).start()
        own_edge(b).start()

    def step(t, _):
        late = jnp.minimum(t // 2, 1)
        lv = late * (1 + lax.rem(t, 2))
        b = (1 - late) * lax.rem(t, 2) + late * (t // 2 - 1)
        buf = lax.rem(lv, 2)


        @pl.when(w > 0)
        def _():
            halo(lv, b, 0).wait_recv()

        @pl.when(w < NW - 1)
        def _():
            halo(lv, b, 1).wait_recv()

        unpack_halo(lv, b, buf)
        apply(lv, b)
        extract(lv + 1, b, 1 - buf, True)

        @pl.when(lv < 2)
        def _():
            send_halo(lv + 1, b)
            shift_own(b, 1 - buf)

        @pl.when(lv == 2)
        def _():
            @pl.when(w > 0)
            def _():
                halo(3, b, 1).start()

            main_copy(b, 2 * qme + 1 - gme, n).start()
            own_main(b).start()

        return 0

    lax.fori_loop(0, 3 * NB, step, 0)

    def own_coef(p, _):
        src = pl.multiple_of(p * (Q * 16) + qme * 16 + 8 * gme, 8)
        k5[pl.ds(pl.multiple_of(p * 8, 8), 8), :] = 0.5 * cv[pl.ds(src, 8), :]
        return 0

    def own_forward(p, _):
        src = pl.multiple_of(p * (Q * FR_) + qme * FR_ + 8 + 8 * gme, 8)
        k5[pl.ds(pl.multiple_of(288 + p * 8, 8), 8), :] = fv[pl.ds(src, 8), :]
        return 0

    lax.fori_loop(0, 36, own_coef, 0, unroll=6)
    lax.fori_loop(0, 144, own_forward, 0, unroll=8)

    for b in range(NB):
        edges(b)
    for b in range(NB):
        for d in range(1, NN):
            main_copy(b, n, lax.rem(n + d, NN)).wait_recv()
        own_main(b).wait()

    def split(v):
        hi = v.astype(BF16)
        return hi, (v - hi.astype(F32)).astype(BF16)

    def fill(ref, slot, at):
        for j in range(J):
            for r in range(8):
                col = pl.ds((j * 8 + r) * 128, 128)
                v = jnp.concatenate(
                    [ref[pl.ds((k * PL + j) * slot + r, 8, stride=J * slot), :] for k in range(NN)], axis=0)
                hi, lo = split(v)
                s[pl.ds(at, 64), col] = hi
                s[pl.ds(at + 64, 64), col] = lo

    def products(at):
        total = jnp.zeros((128, 128), F32)
        for k in range(12):
            col = pl.ds(k * 512, 512)
            total = total + lax.dot_general(
                s[pl.ds(0, 128), col], s[pl.ds(at, 128), col], (((1,), (1,)), ((), ())), preferred_element_type=F32)
        both = total[0:64] + total[64:128]
        return (both + pltpu.roll(both, 64, 1)) / UNKNOWNS

    fill(mc, 16, 0)
    a0[...] = products(0)

    def piece1(dst, sender):
        return pltpu.make_async_remote_copy(
            src_ref=a0.at[pl.ds(pl.multiple_of(dst * 8, 8), 8)], dst_ref=a1.at[sender], send_sem=a1s.at[dst],
            recv_sem=a1r.at[sender], device_id=(w, dst), device_id_type=MESH)

    def piece2(dst, sender):
        return pltpu.make_async_remote_copy(
            src_ref=ps, dst_ref=a2.at[sender], send_sem=a2s.at[dst], recv_sem=a2r.at[sender],
            device_id=(dst, n), device_id_type=MESH)

    def piece3(dst, sender):
        return pltpu.make_async_remote_copy(
            src_ref=pt, dst_ref=a3.at[sender], send_sem=a3s.at[dst], recv_sem=a3r.at[sender],
            device_id=(w, dst), device_id_type=MESH)

    def whole1(dst, sender):
        return pltpu.make_async_remote_copy(
            src_ref=z0, dst_ref=z1.at[sender], send_sem=z1s.at[dst], recv_sem=z1r.at[sender],
            device_id=(w, dst), device_id_type=MESH)

    def whole2(dst, sender):
        return pltpu.make_async_remote_copy(
            src_ref=zp, dst_ref=z2.at[sender], send_sem=z2s.at[dst], recv_sem=z2r.at[sender],
            device_id=(dst, n), device_id_type=MESH)

    def exchange(piece, count, me):
        for d in range(1, count):
            piece(lax.rem(me + d, count), me).start()

    def collect(piece, count, me):
        for d in range(1, count):
            piece(me, lax.rem(me + d, count)).wait_recv()

    def added(ref, count):
        terms = [ref[k] for k in range(count)]
        while len(terms) > 1:
            terms = [terms[k] + terms[k + 1] for k in range(0, len(terms), 2)]
        return terms[0]

    def unpack(b, src):
        base = pl.multiple_of((src * PL + b * PB) * 16, 8)
        pack = epr[b, src, pl.ds(ER, 8), :]
        for p in range(PB):
            v = mc[pl.ds(base + p * 16, 8), :]
            sides = pltpu.roll(pack, 127 - 2 * p, 1)
            mr[pl.ds(base + p * 16, 8), :] = jnp.where(lane == 127, sides, pltpu.roll(v, 127, 1))
            ml[pl.ds(base + p * 16, 8), :] = jnp.where(lane == 0, sides, pltpu.roll(v, 1, 1))
        for k, (first, cnt) in enumerate(groups(PB)):
            h = epr[b, src, pl.ds(first, cnt), :]
            there = pl.ds(base + first * 16 + 8, cnt, stride=16)
            mc[there, :] = h
            mask = lanes(cnt)
            sides = pltpu.roll(pack, 63 - 2 * k, 1)[0:cnt]
            mr[there, :] = jnp.where(mask == 127, sides, pltpu.roll(h, 127, 1))
            ml[there, :] = jnp.where(mask == 0, sides, pltpu.roll(h, 1, 1))

    half_stencil = ((mc, 0), (mr, 0), (ml, 1), (mc, 1), (mr, 1))

    def half_apply(b, src):
        base = pl.multiple_of((src * PL + b * PB) * 16, 8)
        wbase = pl.multiple_of((src * PL + b * PB) * 8, 8)
        acc = [[None] * J for _ in range(MB)]
        for f, (ref, dr) in enumerate(half_stencil):
            for j in range(J):
                vs = [ref[pl.ds(base + (m * J + j) * 16 + dr, 8), :] for m in range(MB)]
                for i in range(J):
                    cf = k5[pl.ds((f * 36 + i * J + j) * 8, 8), :]
                    for m in range(MB):
                        term = cf * vs[m]
                        acc[m][i] = term if acc[m][i] is None else acc[m][i] + term
        for m in range(MB):
            for i in range(J):
                wm[pl.ds(wbase + (m * J + i) * 8, 8), :] = acc[m][i]

    def meet(t, _):
        b, d = t // NN, lax.rem(t, NN)
        src = lax.rem(n + d, NN)

        @pl.when(d == 0)
        def _():
            own_edge(b).wait()

        @pl.when(d > 0)
        def _():
            edge_copy(b, n, src).wait_recv()

        unpack(b, src)
        half_apply(b, src)
        return 0

    def meet_half(half):
        count = NB * NN // 2
        lax.fori_loop(half * count, (half + 1) * count, meet, 0)

    exchange(piece1, NN, n)
    a1[n] = a0[pl.ds(pl.multiple_of(n * 8, 8), 8), :]
    meet_half(0)
    collect(piece1, NN, n)
    ps[...] = added(a1, NN)
    exchange(piece2, NW, w)
    a2[w] = ps[...]
    meet_half(1)
    collect(piece2, NW, w)
    pt[...] = added(a2, NW)
    exchange(piece3, NN, n)
    a3[n] = pt[...]
    fill(wm, 8, 128)
    other = products(128)
    z0[...] = jnp.where(lanes(32) < 64, other[0:32], other[32:64])
    collect(piece3, NN, n)
    gram = jnp.concatenate([a3[k] for k in range(NN)], axis=0)
    exchange(whole1, NN, n)
    z1[n] = z0[...]

    lane64 = lanes(64)
    row64 = lax.broadcasted_iota(jnp.int32, (64, 128), 0)
    work = jnp.where(lane64 < 64, gram, (lane64 - 64 == row64).astype(F32))
    finished = []
    for k0 in range(0, 64, 4):
        first = 8 * len(finished)
        rows = row64[first:]
        column = [jnp.broadcast_to(work[:, k0 + t:k0 + t + 1], work.shape) for t in range(4)]
        line = [work[k0 + t - first:k0 + t - first + 1, :] for t in range(4)]
        for t in range(4):
            at = k0 + t - first
            factor = jnp.where(rows > k0 + t, column[t] * (1.0 / column[t][at:at + 1, :]), 0.0)
            for u in range(t + 1, 4):
                column[u] = column[u] - factor * column[u][at:at + 1, :]
                line[u] = line[u] - factor[at + u - t:at + u - t + 1, :] * line[t]
            work = work - factor * line[t]
        if k0 % 8 == 4:
            finished.append(work[0:8])
            work = work[8:]
    work = jnp.concatenate(finished, axis=0)
    diag = jnp.sum(jnp.where(lane64 == row64, work, 0.0), axis=1, keepdims=True)
    work = work * lax.rsqrt(diag)
    turned = pltpu.roll(work, 64, 1)
    twice = jnp.where(lane64 < 64, turned, work)
    mhi, mlo = split(twice)
    mix = jnp.concatenate([mhi, mlo], axis=0)

    collect(whole1, NN, n)
    zp[...] = added(z1, NN)
    exchange(whole2, NW, w)
    z2[w] = zp[...]

    def back(h, dst):
        return pltpu.make_async_remote_copy(
            src_ref=rb5.at[dst, :, pl.ds(3 * h, 3)],
            dst_ref=out.at[:, pl.ds(3 * h, 3), pl.ds(pl.multiple_of(8 * gme, 8), 8), pl.ds(pl.multiple_of(128 * qme, 128), 128)],
            send_sem=bss.at[h, dst], recv_sem=brs.at[h, n], device_id=(w, dst), device_id_type=MESH)

    def back_arrival(h, sender):
        return pltpu.make_async_remote_copy(
            src_ref=rb5.at[sender, :, pl.ds(3 * h, 3)],
            dst_ref=out.at[:, pl.ds(3 * h, 3), pl.ds(pl.multiple_of(8 * lax.rem(sender, 2), 8), 8),
                           pl.ds(pl.multiple_of(128 * (sender // 2), 128), 128)],
            send_sem=bss.at[h, sender], recv_sem=brs.at[h, sender], device_id=(w, sender), device_id_type=MESH)

    def own_back(h):
        return pltpu.make_async_copy(
            rb5.at[n, :, pl.ds(3 * h, 3)],
            out.at[:, pl.ds(3 * h, 3), pl.ds(pl.multiple_of(8 * gme, 8), 8), pl.ds(pl.multiple_of(128 * qme, 128), 128)],
            locs.at[2 * NB + h])

    for tile in range(24):
        col = pl.ds(tile * 256, 256)
        both = jnp.dot(mix, s[pl.ds(0, 128), col], preferred_element_type=F32)
        basis = both[0:64] + both[64:128]
        for half in range(2):
            j, r = divmod(tile * 2 + half, 8)
            for k in range(NN):
                rb[pl.ds((k * PL + j) * 8 + r, 8, stride=J * 8), :] = basis[8 * k:8 * k + 8, 128 * half:128 * half + 128]
        if tile % 12 == 11:
            for d in (4, 3, 5, 2, 6, 7, 1):
                back(tile // 12, lax.rem(n + d, NN)).start()
            own_back(tile // 12).start()


    collect(whole2, NW, w)
    other = added(z2, NW)
    other = jnp.concatenate([other, pltpu.roll(other, 64, 1)], axis=0)

    minv = jnp.where(lane64 < 64, turned, 0.0)[:, 0:64]
    zmat = other[:, 0:64]
    half = jnp.dot(minv, zmat, precision=HIGHEST, preferred_element_type=F32) + lax.dot_general(
        minv, zmat, (((1,), (1,)), ((), ())), precision=HIGHEST, preferred_element_type=F32)
    pv[...] = lax.dot_general(half, minv, (((1,), (1,)), ((), ())), precision=HIGHEST, preferred_element_type=F32)

    projected = pltpu.make_async_copy(pv, proj, locs.at[2 * NB + 2])
    projected.start()
    projected.wait()

    for lv in range(3):
        for b in range(NB):
            @pl.when(w < NW - 1)
            def _():
                halo(lv, b, 0).wait_send()
    for lv in range(4):
        for b in range(NB):
            @pl.when(w > 0)
            def _():
                halo(lv, b, 1).wait_send()

    @pl.when(w < NW - 1)
    def _():
        coef_halo.wait_send()

    for d in range(1, NN):
        dst = lax.rem(n + d, NN)
        for b in range(NB):
            main_copy(b, dst, n).wait_send()
            edge_copy(b, dst, n).wait_send()
        piece1(dst, n).wait_send()
        piece3(dst, n).wait_send()
        whole1(dst, n).wait_send()
    for d in range(1, NW):
        piece2(lax.rem(w + d, NW), w).wait_send()
        whole2(lax.rem(w + d, NW), w).wait_send()
    for h in range(2):
        own_back(h).wait()
        for d in range(1, NN):
            back(h, lax.rem(n + d, NN)).wait_send()
            back_arrival(h, lax.rem(n + d, NN)).wait_recv()


def hand_over(basis, projected, basis_out, projected_out):
    basis_out[...] = basis[...]
    projected_out[...] = projected[...]


def local(start_block, center_block, forward_blocks, filter_cut, filter_top):
    dma = pltpu.SemaphoreType.DMA
    vm = lambda *shape: pltpu.VMEM(shape, F32)
    anyspace = pl.BlockSpec(memory_space=pl.ANY)
    block = pl.BlockSpec((2, J, 16, 512), lambda k: (k, 0, 0, 0))
    small = pl.BlockSpec((64, 64), lambda k: (0, 0))
    basis, projected = pl.pallas_call(
        kernel,
        out_shape=(jax.ShapeDtypeStruct((ML, J, 16, 512), F32), jax.ShapeDtypeStruct((64, 64), F32)),
        in_specs=[anyspace] * 5,
        out_specs=(anyspace, anyspace),
        scratch_shapes=[
            pltpu.SMEM((1,), F32), pltpu.SMEM((1,), F32),
            vm(2 * VSZ, 128), vm(VSZ, 128), vm(VSZ, 128),
            vm(36 * Q * 16, 128), vm(144 * Q * FR_, 128), vm(108 * Q * FR_, 128),
            vm(Q, 112, 128), vm(Q, 112, 128),
            vm(4, NB, 2, Q * PB, 128), vm(4, NB, 2, Q * PB, 128),
            vm(NB, NN, ER + 8, 128), vm(NB, NN, ER + 8, 128),
            vm(NN * PL * 16, 128), vm(NN * PL * 16, 128), vm(NN * PL * 16, 128),
            vm(180 * 8, 128), vm(NN * PL * 8, 128), pltpu.VMEM((256, 6144), BF16), vm(NN * PL * 8, 128),
            vm(64, 128), vm(NN, 8, 128), vm(8, 128), vm(NW, 8, 128), vm(8, 128), vm(NN, 8, 128), vm(64, 64),
            vm(32, 128), vm(NN, 32, 128), vm(32, 128), vm(NW, 32, 128),
            dma((14,)), dma((4, NB, 2)), dma((4, NB, 2)), dma(()), dma(()),
            dma((NB, NN)), dma((NB, NN)), dma((NB, NN)), dma((NB, NN)),
            dma((NN,)), dma((NN,)), dma((NW,)), dma((NW,)), dma((NN,)), dma((NN,)),
            dma((NN,)), dma((NN,)), dma((NW,)), dma((NW,)), dma((2, NN)), dma((2, NN)),
            dma((2 * NB + 3,)),
        ],
        compiler_params=pltpu.CompilerParams(
            collective_id=0, has_side_effects=True, vmem_limit_bytes=60 * 1024 * 1024),
    )(start_block, center_block, forward_blocks, filter_cut, filter_top)
    return pl.pallas_call(
        hand_over,
        out_shape=(jax.ShapeDtypeStruct(basis.shape, F32), jax.ShapeDtypeStruct(projected.shape, F32)),
        grid=(4,),
        in_specs=[block, small],
        out_specs=(block, small),
    )(basis, projected)


def solution(mesh):
    in_specs = (
        P("narrow", None, "wide", None),
        P(None, None, "wide", None),
        P(None, None, None, "wide", None),
        P(),
        P(),
    )
    out_specs = (P("narrow", None, "wide", None), P())
    return jax.shard_map(local, mesh=mesh, in_specs=in_specs, out_specs=out_specs, check_vma=False)
```

time: 122 us -> 109 us (0.89)
  Pallas kernels: 117 us -> 107 us
  local copies, waits for them, and re-layouts: 3.39 us -> 0 us
    pallas_call x1, Pallas kernels: 117 us -> 103 us  [local(): pl.pallas_call(kernel, out_shape=(jax.ShapeDtypeStruct((ML, J, 16, 512),...]
    pallas_call x0 -> x1, Pallas kernels: none -> 3.58 us  [local(): pl.pallas_call(hand_over, out_shape=(jax.ShapeDtypeStruct(basis.shape, F3...]
    unnamed x4 -> x0, local copies, waits for them, and re-layouts: 3.39 us -> none
where the time goes in v1:
time: 109 us
  Pallas kernels  107 us (98%)
  between operations  1.93 us (2%)
    pallas_call x1, Pallas kernels, local(): pl.pallas_call(kernel, out_shape=(jax.ShapeDtypeStruct((ML, J, 16, 512),...  103 us
    pallas_call x1, Pallas kernels, local(): pl.pallas_call(hand_over, out_shape=(jax.ShapeDtypeStruct(basis.shape, F3...  3.58 us

profile of v1, /device:TPU:0, one launch (start us, length us, event | category | flops | bytes accessed | tf_op | source)
XLA Modules:
  0.0 108.8 jit_solution(14846614636610916090)
XLA Ops:
  1.9 103.3 %shard_map.68 = (f32[8,6,16,512]{3,2,1,0:T(8,128)}, f32[64,64]{1,0:T(8,128)}) custom-call(f32[8,6,16,512]{3,2,1,0:T(8,128)} %x.1, f32[6,6,16,512]{3,2,1,0:T(8,128)} %cen.1, f32[4,6,6,16,512]{4,3,2,1,0:T(8,128)} %fwd.1, f32[1]{0:T(128)S(6)} %copy.7.cut_hbm, f32[1]{0:T(128)S(6)} %copy.8.top_hbm), custom_call_target="tpu_custom_call" | custom-call | tf_op jit(solution)/shard_map/pallas_call | solution.py:625
  105.2 3.6 %shard_map.69 = (f32[8,6,16,512]{3,2,1,0:T(8,128)}, f32[64,64]{1,0:T(8,128)}) custom-call(f32[8,6,16,512]{3,2,1,0:T(8,128)} %get-tuple-element.4.basis, f32[64,64]{1,0:T(8,128)} %get-tuple-element.5.projected), custom_call_target="tpu_custom_call" | custom-call | tf_op jit(solution)/shard_map/pallas_call | solution.py:650

commit v2 on v1

--- a/solution.py
+++ b/solution.py
@@ -71,7 +71,7 @@
         cl.append(pltpu.make_async_copy(cen.at[:, :, :, col], cv5.at[:, :, q], ldsem.at[4 + q]))
         fl.append(pltpu.make_async_copy(fwd.at[:, :, :, :, col], fv6.at[:, :, :, q, pl.ds(8, 16)], ldsem.at[8 + q]))
     scalars = [pltpu.make_async_copy(cut_hbm, cut, ldsem.at[12]), pltpu.make_async_copy(top_hbm, top, ldsem.at[13])]
-    for c in fl + xl + cl + scalars:
+    for c in xl + fl + cl + scalars:
         c.start()
 
     zero = jnp.zeros((8, 128), F32)
@@ -85,6 +85,20 @@
         return 0
 
     lax.fori_loop(0, PL * Q, clear, 0, unroll=8)
+
+    def clear_rows(p, _):
+        for ref in (vc, vl, vr):
+            for at in (0, 24):
+                ref[pl.ds(pl.multiple_of(p * VR_, 8) + at, 8), :] = zero
+        return 0
+
+    def clear_coef(p, _):
+        for ref, slot in ((sh, 1), (sh, 2), (fv, 2)):
+            ref[pl.ds(pl.multiple_of(slot * 36 * Q * FR_ + p * FR_, 8), 8), :] = zero
+        return 0
+
+    lax.fori_loop(0, PL * Q, clear_rows, 0, unroll=8)
+    lax.fori_loop(0, 36 * Q, clear_coef, 0, unroll=8)
 
     @pl.when(w == 0)
     def _():
@@ -146,6 +160,13 @@
                 for ref, off, vals in ((vc, buf * VSZ, tiles), (vl, 0, from_left(tiles)), (vr, 0, from_right(tiles))):
                     for q in range(Q):
                         ref[pl.ds(off + base + q * VR_ + row, cnt, stride=Q * VR_), :] = vals[q]
+
+    for c in xl:
+        c.wait()
+    for b in range(NB):
+        extract(0, b, 0, True)
+    for b in range(NB):
+        shift_own(b, 0)
 
     for c in fl:
         c.wait()
@@ -166,34 +187,6 @@
 
         lax.fori_loop(0, 36, body, 0, unroll=12)
 
-    for c in xl:
-        c.wait()
-    for b in range(NB):
-        extract(0, b, 0, True)
-    pl.semaphore_wait(barrier, NN + NW - 2)
-    for b in range(NB):
-        send_halo(0, b)
-
-    coef_halo = pltpu.make_async_remote_copy(
-        src_ref=cs, dst_ref=ch, send_sem=css, recv_sem=crs, device_id=down_dev, device_id_type=MESH)
-
-    @pl.when(w < NW - 1)
-    def _():
-        coef_halo.start()
-
-    for b in range(NB):
-        shift_own(b, 0)
-
-    @pl.when(w > 0)
-    def _():
-        coef_halo.wait_recv()
-
-    for at, cnt in groups(36):
-        for f, ref, slot, move in ((1, sh, 1, from_right), (2, fv, 2, None), (3, sh, 2, from_left)):
-            tiles = [ch[q, pl.ds((f - 1) * 36 + at, cnt), :] for q in range(Q)]
-            tiles = tiles if move is None else move(tiles)
-            for q in range(Q):
-                ref[pl.ds(((slot * 36 + at) * Q + q) * FR_ + 7, cnt, stride=Q * FR_), :] = tiles[q]
     for c in cl + scalars:
         c.wait()
 
@@ -218,9 +211,9 @@
             mc4.at[n, pl.ds(b * PB, PB), pl.ds(0, 8)], locs.at[b])
 
     def apply(lv, b):
-        cur = lax.rem(lv, 2) * VSZ
+        cur = 0 if isinstance(lv, int) else lax.rem(lv, 2) * VSZ
         nxt = VSZ - cur
-        scale = jnp.where(lv == 0, 1.0, 2.0) / half_width
+        scale = (1.0 if isinstance(lv, int) else 2.0) / half_width
         vb = b * (PB * Q * VR_)
 
         def body(k, _):
@@ -248,10 +241,11 @@
                         there = pl.ds(pl.multiple_of(off + nxt, 8) + at, 8)
                         vc[there, :] = (acc[m][i] - middle * here) * scale - vc[there, :]
 
-            @pl.when((lv == 2) & (k < Q - 1))
-            def _():
-                for g in range(2):
-                    main_copy(b, 2 * q + g, n).start()
+            if not isinstance(lv, int):
+                @pl.when((lv == 2) & (k < Q - 1))
+                def _():
+                    for g in range(2):
+                        main_copy(b, 2 * q + g, n).start()
 
             return 0
 
@@ -303,9 +297,7 @@
         own_edge(b).start()
 
     def step(t, _):
-        late = jnp.minimum(t // 2, 1)
-        lv = late * (1 + lax.rem(t, 2))
-        b = (1 - late) * lax.rem(t, 2) + late * (t // 2 - 1)
+        lv, b = 1 + lax.rem(t, 2), t // 2
         buf = lax.rem(lv, 2)
 
 
@@ -321,7 +313,7 @@
         apply(lv, b)
         extract(lv + 1, b, 1 - buf, True)
 
-        @pl.when(lv < 2)
+        @pl.when(lv == 1)
         def _():
             send_halo(lv + 1, b)
             shift_own(b, 1 - buf)
@@ -337,7 +329,69 @@
 
         return 0
 
-    lax.fori_loop(0, 3 * NB, step, 0)
+    apply(0, 0)
+
+    pl.semaphore_wait(barrier, NN + NW - 2)
+    for b in range(NB):
+        send_halo(0, b)
+
+    coef_halo = pltpu.make_async_remote_copy(
+        src_ref=cs, dst_ref=ch, send_sem=css, recv_sem=crs, device_id=down_dev, device_id_type=MESH)
+
+    @pl.when(w < NW - 1)
+    def _():
+        coef_halo.start()
+
+    apply(0, 1)
+
+    for b in range(NB):
+        @pl.when(w > 0)
+        def _():
+            halo(0, b, 0).wait_recv()
+
+        @pl.when(w < NW - 1)
+        def _():
+            halo(0, b, 1).wait_recv()
+
+    @pl.when(w > 0)
+    def _():
+        coef_halo.wait_recv()
+
+    def outside(side, j):
+        return [jnp.concatenate(
+            [hr[0, b, side, pl.ds(q * PB + j, MB, stride=J), :] for b in range(NB)], axis=0) for q in range(Q)]
+
+    def add_row(i, q, row, extra):
+        there = pl.ds(VSZ + (i * Q + q) * VR_ + row, ML, stride=J * Q * VR_)
+        vc[there, :] = vc[there, :] + extra * (1.0 / half_width)
+
+    above = [outside(0, j) for j in range(J)]
+    for i in range(J):
+        parts = []
+        for f in range(3):
+            parts.append([sum(ch[q, pl.ds(f * 36 + j * J + i, 1), :] * above[j][q] for j in range(J)) for q in range(Q)])
+        left, right = from_right(parts[0]), from_left(parts[2])
+        for q in range(Q):
+            add_row(i, q, 8, left[q] + parts[1][q] + right[q])
+    below = [outside(1, j) for j in range(J)]
+    moved = [[from_left(t) for t in below], below, [from_right(t) for t in below]]
+    for i in range(J):
+        for q in range(Q):
+            add_row(i, q, 23, sum(
+                cs[q, pl.ds(f * 36 + i * J + j, 1), :] * moved[f][j][q] for f in range(3) for j in range(J)))
+    for b in range(NB):
+        extract(1, b, 1, True)
+        send_halo(1, b)
+    for b in range(NB):
+        shift_own(b, 1)
+    for at, cnt in groups(36):
+        for f, ref, slot, move in ((1, sh, 1, from_right), (2, fv, 2, None), (3, sh, 2, from_left)):
+            tiles = [ch[q, pl.ds((f - 1) * 36 + at, cnt), :] for q in range(Q)]
+            tiles = tiles if move is None else move(tiles)
+            for q in range(Q):
+                ref[pl.ds(((slot * 36 + at) * Q + q) * FR_ + 7, cnt, stride=Q * FR_), :] = tiles[q]
+
+    lax.fori_loop(0, 2 * NB, step, 0)
 
     def own_coef(p, _):
         src = pl.multiple_of(p * (Q * 16) + qme * 16 + 8 * gme, 8)
@@ -533,21 +587,21 @@
 
     def back(h, dst):
         return pltpu.make_async_remote_copy(
-            src_ref=rb5.at[dst, :, pl.ds(3 * h, 3)],
-            dst_ref=out.at[:, pl.ds(3 * h, 3), pl.ds(pl.multiple_of(8 * gme, 8), 8), pl.ds(pl.multiple_of(128 * qme, 128), 128)],
+            src_ref=rb5.at[dst, :, pl.ds(2 * h, 2)],
+            dst_ref=out.at[:, pl.ds(2 * h, 2), pl.ds(pl.multiple_of(8 * gme, 8), 8), pl.ds(pl.multiple_of(128 * qme, 128), 128)],
             send_sem=bss.at[h, dst], recv_sem=brs.at[h, n], device_id=(w, dst), device_id_type=MESH)
 
     def back_arrival(h, sender):
         return pltpu.make_async_remote_copy(
-            src_ref=rb5.at[sender, :, pl.ds(3 * h, 3)],
-            dst_ref=out.at[:, pl.ds(3 * h, 3), pl.ds(pl.multiple_of(8 * lax.rem(sender, 2), 8), 8),
+            src_ref=rb5.at[sender, :, pl.ds(2 * h, 2)],
+            dst_ref=out.at[:, pl.ds(2 * h, 2), pl.ds(pl.multiple_of(8 * lax.rem(sender, 2), 8), 8),
                            pl.ds(pl.multiple_of(128 * (sender // 2), 128), 128)],
             send_sem=bss.at[h, sender], recv_sem=brs.at[h, sender], device_id=(w, sender), device_id_type=MESH)
 
     def own_back(h):
         return pltpu.make_async_copy(
-            rb5.at[n, :, pl.ds(3 * h, 3)],
-            out.at[:, pl.ds(3 * h, 3), pl.ds(pl.multiple_of(8 * gme, 8), 8), pl.ds(pl.multiple_of(128 * qme, 128), 128)],
+            rb5.at[n, :, pl.ds(2 * h, 2)],
+            out.at[:, pl.ds(2 * h, 2), pl.ds(pl.multiple_of(8 * gme, 8), 8), pl.ds(pl.multiple_of(128 * qme, 128), 128)],
             locs.at[2 * NB + h])
 
     for tile in range(24):
@@ -558,10 +612,10 @@
             j, r = divmod(tile * 2 + half, 8)
             for k in range(NN):
                 rb[pl.ds((k * PL + j) * 8 + r, 8, stride=J * 8), :] = basis[8 * k:8 * k + 8, 128 * half:128 * half + 128]
-        if tile % 12 == 11:
+        if tile % 8 == 7:
             for d in (4, 3, 5, 2, 6, 7, 1):
-                back(tile // 12, lax.rem(n + d, NN)).start()
-            own_back(tile // 12).start()
+                back(tile // 8, lax.rem(n + d, NN)).start()
+            own_back(tile // 8).start()
 
 
     collect(whole2, NW, w)
@@ -574,7 +628,7 @@
         minv, zmat, (((1,), (1,)), ((), ())), precision=HIGHEST, preferred_element_type=F32)
     pv[...] = lax.dot_general(half, minv, (((1,), (1,)), ((), ())), precision=HIGHEST, preferred_element_type=F32)
 
-    projected = pltpu.make_async_copy(pv, proj, locs.at[2 * NB + 2])
+    projected = pltpu.make_async_copy(pv, proj, locs.at[2 * NB + 3])
     projected.start()
     projected.wait()
 
@@ -604,24 +658,30 @@
     for d in range(1, NW):
         piece2(lax.rem(w + d, NW), w).wait_send()
         whole2(lax.rem(w + d, NW), w).wait_send()
-    for h in range(2):
+    for h in range(3):
         own_back(h).wait()
         for d in range(1, NN):
             back(h, lax.rem(n + d, NN)).wait_send()
             back_arrival(h, lax.rem(n + d, NN)).wait_recv()
 
 
-def hand_over(basis, projected, basis_out, projected_out):
-    basis_out[...] = basis[...]
-    projected_out[...] = projected[...]
+def hand_over(basis, projected, basis_out, projected_out, held, small, sems):
+    pairs = [(basis.at[m], held.at[m], basis_out.at[m]) for m in range(ML)] + [(projected, small, projected_out)]
+    arriving = [pltpu.make_async_copy(src, mid, sems.at[0, k]) for k, (src, mid, _) in enumerate(pairs)]
+    leaving = [pltpu.make_async_copy(mid, dst, sems.at[1, k]) for k, (_, mid, dst) in enumerate(pairs)]
+    for c in arriving:
+        c.start()
+    for c, d in zip(arriving, leaving):
+        c.wait()
+        d.start()
+    for d in leaving:
+        d.wait()
 
 
 def local(start_block, center_block, forward_blocks, filter_cut, filter_top):
     dma = pltpu.SemaphoreType.DMA
     vm = lambda *shape: pltpu.VMEM(shape, F32)
     anyspace = pl.BlockSpec(memory_space=pl.ANY)
-    block = pl.BlockSpec((2, J, 16, 512), lambda k: (k, 0, 0, 0))
-    small = pl.BlockSpec((64, 64), lambda k: (0, 0))
     basis, projected = pl.pallas_call(
         kernel,
         out_shape=(jax.ShapeDtypeStruct((ML, J, 16, 512), F32), jax.ShapeDtypeStruct((64, 64), F32)),
@@ -641,8 +701,8 @@
             dma((14,)), dma((4, NB, 2)), dma((4, NB, 2)), dma(()), dma(()),
             dma((NB, NN)), dma((NB, NN)), dma((NB, NN)), dma((NB, NN)),
             dma((NN,)), dma((NN,)), dma((NW,)), dma((NW,)), dma((NN,)), dma((NN,)),
-            dma((NN,)), dma((NN,)), dma((NW,)), dma((NW,)), dma((2, NN)), dma((2, NN)),
-            dma((2 * NB + 3,)),
+            dma((NN,)), dma((NN,)), dma((NW,)), dma((NW,)), dma((3, NN)), dma((3, NN)),
+            dma((2 * NB + 4,)),
         ],
         compiler_params=pltpu.CompilerParams(
             collective_id=0, has_side_effects=True, vmem_limit_bytes=60 * 1024 * 1024),
@@ -650,9 +710,9 @@
     return pl.pallas_call(
         hand_over,
         out_shape=(jax.ShapeDtypeStruct(basis.shape, F32), jax.ShapeDtypeStruct(projected.shape, F32)),
-        grid=(4,),
-        in_specs=[block, small],
-        out_specs=(block, small),
+        in_specs=[anyspace] * 2,
+        out_specs=(anyspace, anyspace),
+        scratch_shapes=[vm(ML, J, 16, 512), vm(64, 64), dma((2, ML + 1))],
     )(basis, projected)
 
 

time: 109 us -> 106 us (0.972)
  Pallas kernels: 107 us -> 104 us
    pallas_call x1, Pallas kernels: 103 us -> 102 us  [local(): pl.pallas_call(kernel, out_shape=(jax.ShapeDtypeStruct((ML, J, 16, 512),...]
    pallas_call x1, Pallas kernels: 3.58 us -> 2.31 us  [local(): pl.pallas_call(hand_over, out_shape=(jax.ShapeDtypeStruct(basis.shape, F3...]
where the time goes in v2:
time: 106 us
  Pallas kernels  104 us (98%)
  between operations  2.09 us (2%)
    pallas_call x1, Pallas kernels, local(): pl.pallas_call(kernel, out_shape=(jax.ShapeDtypeStruct((ML, J, 16, 512),...  102 us
    pallas_call x1, Pallas kernels, local(): pl.pallas_call(hand_over, out_shape=(jax.ShapeDtypeStruct(basis.shape, F3...  2.31 us

profile of v2, /device:TPU:0, one launch (start us, length us, event | category | flops | bytes accessed | tf_op | source)
XLA Modules:
  0.0 106.1 jit_solution(2188637839137032685)
XLA Ops:
  1.9 101.7 %shard_map.68 = (f32[8,6,16,512]{3,2,1,0:T(8,128)}, f32[64,64]{1,0:T(8,128)}) custom-call(f32[8,6,16,512]{3,2,1,0:T(8,128)} %x.1, f32[6,6,16,512]{3,2,1,0:T(8,128)} %cen.1, f32[4,6,6,16,512]{4,3,2,1,0:T(8,128)} %fwd.1, f32[1]{0:T(128)S(6)} %copy.7.cut_hbm, f32[1]{0:T(128)S(6)} %copy.8.top_hbm), custom_call_target="tpu_custom_call" | custom-call | tf_op jit(solution)/shard_map/pallas_call | solution.py:685
  103.6 2.3 %shard_map.69 = (f32[8,6,16,512]{3,2,1,0:T(8,128)}, f32[64,64]{1,0:T(8,128)}) custom-call(f32[8,6,16,512]{3,2,1,0:T(8,128)} %get-tuple-element.4.basis, f32[64,64]{1,0:T(8,128)} %get-tuple-element.5.projected), custom_call_target="tpu_custom_call" | custom-call | tf_op jit(solution)/shard_map/pallas_call | solution.py:710
